TPU v7x, 32 devices: a whole 2x2x4 slice. The times are simulated.
32 devices in a mesh: expert: 4 (over y, x), tile: 8 (over z, core).
Axes of the slice: x: 2, y: 2, z: 4, core: 2. Of those that a mesh axis runs over, the one named last changes fastest.
Arguments:
- activations: bfloat16 [1536, 6144], P(('expert', 'tile')), may hold values from -40 to 40
- expert_ids: int32 [1536, 2], P(('expert', 'tile')), may hold values from 0 to 3, all different within a row; in each aligned block of 48 rows (0 to 47, 48 to 95, ...) at most 48 rows name the same one
Outputs:
- hessian: float32 [4, 6144, 6144], P('expert', 'tile')
- panels: float32 [4, 6144, 1536], P('expert', 'tile')
Inputs may be any that keep to these rules, and one draw needn't show every extreme that they name: `expert_ids`: each row names 2 different experts; within the rows of one device no expert is named more than 48 times, a bound that some block reaches; every expert is named by some row.
All inputs are finite; a program needn't handle non-finite values.
Results may differ from a plain program's by a relative error of at most 0.0003.
Values may be sent and summed in bfloat16 or wider, within the bound.
A program may use at most 256 MiB of HBM per device.

v0:
```python
import jax
import jax.numpy as jnp
from jax import lax
from jax.sharding import PartitionSpec as P

PANEL = 768


damp_fraction = 0.01


def from_root(value, axis, source):
    kept = jnp.where(lax.axis_index(axis) == source, value, 0).astype(value.dtype)
    return lax.psum(kept, axis)


def local(activations, expert_ids):
    tile_count = lax.axis_size("tile")
    group_count = lax.axis_size("expert")
    token_count = activations.shape[0]
    feature_width = activations.shape[1]
    capacity = 2 * token_count * expert_ids.shape[1] // group_count
    rows_device = feature_width // tile_count
    tile_index = lax.axis_index("tile")
    expert_iota = jnp.arange(group_count, dtype=jnp.int32)
    global_rows = tile_index * rows_device + jnp.arange(rows_device, dtype=jnp.int32)
    routed = jnp.sum((expert_ids[None][..., None] == expert_iota).astype(jnp.int32), axis=2)
    slot_index = jnp.cumsum(routed, axis=1) - 1
    slot_iota = jnp.arange(capacity, dtype=jnp.int32)
    selector = (routed[..., None] > 0) & (slot_index[..., None] == slot_iota)
    packed = jnp.einsum(
        "nkes,nkd->ensd",
        selector.astype(jnp.bfloat16),
        activations[None],
        preferred_element_type=jnp.float32,
    ).astype(jnp.bfloat16)
    flags = jnp.transpose(jnp.sum(selector.astype(jnp.float32), axis=1), (1, 0, 2)).astype(
        jnp.bfloat16
    )
    send_rows = packed
    send_flags = flags
    send_rows = send_rows.reshape(group_count, capacity, feature_width)
    send_flags = send_flags.reshape(group_count, capacity)
    received_rows, received_flags = (
        lax.all_to_all(send_rows, "expert", split_axis=0, concat_axis=0, tiled=True),
        lax.all_to_all(send_flags, "expert", split_axis=0, concat_axis=0, tiled=True),
    )
    accumulate_received_rows = lax.all_gather(
        received_rows.reshape(group_count * capacity, feature_width), "tile", axis=0, tiled=True
    )
    accumulate_received_flags = lax.all_gather(
        received_flags.reshape(group_count * capacity), "tile", axis=0, tiled=True
    )
    own_columns = lax.dynamic_slice_in_dim(
        accumulate_received_rows, tile_index * rows_device, rows_device, 1
    )
    total = jnp.einsum(
        "tr,tc->rc", own_columns, accumulate_received_rows, preferred_element_type=jnp.float32
    )
    expert_count = jnp.sum(accumulate_received_flags.astype(jnp.float32))
    hessian = total * (2.0 / expert_count)
    diag_mask = global_rows[:, None] == jnp.arange(feature_width, dtype=jnp.int32)[None, :]
    diag_total = lax.psum(jnp.sum(jnp.where(diag_mask, hessian, jnp.float32(0.0))), "tile")
    damping = damp_fraction * diag_total / feature_width
    hessian = hessian + jnp.where(diag_mask, damping, jnp.float32(0.0))

    def panel_rows_fetch(members, panel_start):
        received_list = []
        for sub_block in range(PANEL // rows_device):
            received_list.append(
                jax.tree.map(
                    lambda part: from_root(part, "tile", panel_start // rows_device + sub_block),
                    members,
                )
            )
        return tuple(
            (
                jnp.concatenate([sent_piece[member] for sent_piece in received_list], axis=0)
                for member in range(len(members))
            )
        )

    factors = []
    for panel in range(2):
        panel_start = panel * PANEL
        panel_block = hessian[:, panel_start : panel_start + PANEL]
        if factors:
            diagonal_rows, earlier_rows = panel_rows_fetch((panel_block, factors[0]), panel_start)
            panel_block = panel_block - jnp.dot(
                factors[0], earlier_rows.T, precision=lax.Precision.HIGHEST
            )
            diagonal_block = diagonal_rows - jnp.dot(
                earlier_rows, earlier_rows.T, precision=lax.Precision.HIGHEST
            )
        else:
            diagonal_block = panel_rows_fetch((panel_block,), panel_start)[0]
        diagonal_factor = jnp.linalg.cholesky(diagonal_block)
        panel_factor = jax.scipy.linalg.solve_triangular(
            diagonal_factor, panel_block.T, lower=True
        ).T
        column_index = panel_start + jnp.arange(PANEL, dtype=jnp.int32)
        lower_mask = global_rows[:, None] >= column_index[None, :]
        factors.append(jnp.where(lower_mask, panel_factor, jnp.float32(0.0)))
    return (hessian[None], jnp.concatenate(factors, axis=1)[None])


def solution(mesh):
    placed = (P(("expert", "tile"), None), P(("expert", "tile"), None))
    return jax.shard_map(
        local,
        mesh=mesh,
        in_specs=placed,
        out_specs=(P("expert", "tile", None), P("expert", "tile", None)),
        check_vma=False,
    )
```

profile of v0, /device:TPU:0, one launch (start us, length us, event | category | flops | bytes accessed | tf_op | source)
XLA Modules:
  0.0 946.3 jit_solution(5320931282133351757)
XLA Ops:
  9.0 33.3 %all_to_all.11 = bf16[4,48,6144]{2,1,0:T(8,128)(2,1)} all-to-all(bf16[4,48,6144]{2,1,0:T(8,128)(2,1)S(1)} %convolution_convert_fusion), channel_id=1, replica_groups=mesh['expert'=4,'tile'=8] {'expert'}, dimensions={0} | all-to-all | bytes 4718592 | tf_op jit(solution)/shard_map/all_to_all | solution.py:45
  43.0 3.2 all-to-all-start.1
  47.6 3.2 all-to-all-done.1
  51.1 14.5 %all-reduce.1 = bf16[1536]{0:T(1024)(128)(2,1)S(1)} all-reduce(bf16[1536]{0:T(1024)(128)(2,1)S(1)} %dynamic-update-slice.25), channel_id=1, replica_groups=mesh['expert'=4,'tile'=8] {'tile'}, use_global_device_ids=true, to_apply=%add.1 | all-reduce | flops 1536 | bytes 6144
  66.9 143.8 %all-gather.2.cloned.1.call-done = bf16[1536,6144]{1,0:T(8,128)(2,1)} async-done(((bf16[192,6144]{1,0:T(8,128)(2,1)}), bf16[1536,6144]{1,0:T(8,128)(2,1)}) %all-gather.2.cloned.1.call-update) | async-done | bytes 18874384 | tf_op jit(solution)/shard_map/all_gather | solution.py:48
  210.7 23.5 %select_reduce_fusion = (f32[]{:T(128)}, f32[768,6144]{0,1:T(8,128)}) fusion(s32[768]{0:T(1024)S(1)} %iota_add_fusion.1, f32[]{:T(128)S(6)} %div.12, bf16[1536,6144]{1,0:T(8,128)(2,1)} %all-gather.2.cloned.1.call-done, s32[]{:T(128)S(6)} %select_n.39), kind=kOutput, calls=%fused_computation.5 | convolution fusion | flops 14514388992 | bytes 40111116 | tf_op jit(solution)/shard_map/tr,tc->rc/dot_general | solution.py:57
  234.3 14.5 %psum.28 = f32[]{:T(128)} all-reduce(f32[]{:T(128)} %get-tuple-element.107), channel_id=1, replica_groups=mesh['expert'=4,'tile'=8] {'tile'}, use_global_device_ids=true, to_apply=%region_5.6 | all-reduce | flops 1 | bytes 8 | tf_op jit(solution)/shard_map/psum | solution.py:63
  249.4 8.2 select_add_fusion
  257.6 6.5 copy-done.2
  264.0 3.4 slice_select_fusion
  267.5 64.9 %all-reduce.6.cloned.1.call-done = f32[768,768]{0,1:T(8,128)} async-done(((f32[768,768]{0,1:T(8,128)}), f32[768,768]{0,1:T(8,128)}) %all-reduce.6.cloned.1.call-update) | async-done | bytes 2359312 | tf_op jit(solution)/shard_map/psum | solution.py:14
  332.4 3.7 copy.40
  336.2 2.0 fusion.1
  339.6 11.7 %cholesky.453 = f32[128,128]{1,0:T(8,128)S(1)} custom-call(f32[128,128]{1,0:T(8,128)S(1)} %cholesky.669), custom_call_target="Cholesky" | custom-call | tf_op jit(solution)/shard_map/jit(cholesky)/cholesky | solution.py:97
  351.5 9.8 %custom-call.41 = f32[1,128,128]{1,2,0:T(8,128)S(1)} custom-call(f32[1,128,128]{2,1,0:T(8,128)S(1)} %get-tuple-element.106), custom_call_target="InvertDiagBlocksLowerTriangular" | custom-call | tf_op jit(solution)/shard_map/jit(cholesky)/cholesky | solution.py:97
  364.1 11.7 %cholesky.472 = f32[128,128]{1,0:T(8,128)S(1)} custom-call(f32[128,128]{1,0:T(8,128)S(1)} %cholesky.673), custom_call_target="Cholesky" | custom-call | tf_op jit(solution)/shard_map/jit(cholesky)/cholesky | solution.py:97
  375.9 10.0 %custom-call.42 = f32[1,128,128]{1,2,0:T(8,128)S(1)} custom-call(f32[1,128,128]{2,1,0:T(8,128)S(1)} %get-tuple-element.103), custom_call_target="InvertDiagBlocksLowerTriangular" | custom-call | tf_op jit(solution)/shard_map/jit(cholesky)/cholesky | solution.py:97
  387.7 11.7 %cholesky.493 = f32[128,128]{1,0:T(8,128)S(1)} custom-call(f32[128,128]{1,0:T(8,128)S(1)} %cholesky.678), custom_call_target="Cholesky" | custom-call | tf_op jit(solution)/shard_map/jit(cholesky)/cholesky | solution.py:97
  400.1 9.8 %custom-call.43 = f32[1,128,128]{1,2,0:T(8,128)S(1)} custom-call(f32[1,128,128]{2,1,0:T(8,128)S(1)} %get-tuple-element.100), custom_call_target="InvertDiagBlocksLowerTriangular" | custom-call | tf_op jit(solution)/shard_map/jit(cholesky)/cholesky | solution.py:97
  411.8 12.1 %cholesky.512 = f32[128,128]{1,0:T(8,128)S(1)} custom-call(f32[128,128]{1,0:T(8,128)S(1)} %cholesky.683), custom_call_target="Cholesky" | custom-call | tf_op jit(solution)/shard_map/jit(cholesky)/cholesky | solution.py:97
  424.7 9.8 %custom-call.44 = f32[1,128,128]{1,2,0:T(8,128)S(1)} custom-call(f32[1,128,128]{2,1,0:T(8,128)S(1)} %get-tuple-element.97), custom_call_target="InvertDiagBlocksLowerTriangular" | custom-call | tf_op jit(solution)/shard_map/jit(cholesky)/cholesky | solution.py:97
  436.3 11.7 %cholesky.531 = f32[128,128]{1,0:T(8,128)S(1)} custom-call(f32[128,128]{1,0:T(8,128)S(1)} %cholesky.688), custom_call_target="Cholesky" | custom-call | tf_op jit(solution)/shard_map/jit(cholesky)/cholesky | solution.py:97
  448.7 9.8 %custom-call.45 = f32[1,128,128]{1,2,0:T(8,128)S(1)} custom-call(f32[1,128,128]{2,1,0:T(8,128)S(1)} %get-tuple-element.94), custom_call_target="InvertDiagBlocksLowerTriangular" | custom-call | tf_op jit(solution)/shard_map/jit(cholesky)/cholesky | solution.py:97
  460.0 11.9 %cholesky.548 = f32[128,128]{1,0:T(8,128)S(1)} custom-call(f32[128,128]{1,0:T(8,128)S(1)} %convolution_subtract_fusion.18), custom_call_target="Cholesky" | custom-call | tf_op jit(solution)/shard_map/jit(cholesky)/cholesky | solution.py:97
  478.6 17.6 %while.4 = (s32[]{:T(128)}, f32[768,768]{1,0:T(8,128)}, s32[6,2]{0,1:T(2,128)S(1)}, f32[6,128,128]{2,1,0:T(8,128)S(1)}, s32[]{:T(128)}) while((s32[]{:T(128)}, f32[768,768]{1,0:T(8,128)}, s32[6,2]{0,1:T(2,128)S(1)}, f32[6,128,128]{2,1,0:T(8,128)S(1)}, s32[]{:T(128)}) %tuple.89), condition=%wide.while_cond, body=%wide.while_body.sunk | while | flops 2 | bytes 131181 | solution.py:98
  479.3 2.2 bitcast_dynamic-update-slice_fusion.4
  482.2 2.2 bitcast_dynamic-update-slice_fusion.4
  485.2 2.2 bitcast_dynamic-update-slice_fusion.4
  488.1 2.2 bitcast_dynamic-update-slice_fusion.4
  491.1 2.2 bitcast_dynamic-update-slice_fusion.4
  494.0 2.2 bitcast_dynamic-update-slice_fusion.4
  496.2 59.0 %custom-call.46 = f32[6,128,128]{1,2,0:T(8,128)S(1)} custom-call(f32[6,128,128]{2,1,0:T(8,128)S(1)} %get-tuple-element.18), custom_call_target="InvertDiagBlocksLowerTriangular" | custom-call | tf_op jit(solution)/shard_map/jit(_solve_triangular)/triangular_solve | solution.py:98
  565.6 2.3 convolution_subtract_fusion.4
  568.4 2.6 broadcast_select_fusion
  571.1 16.0 %fusion.138 = f32[1,768,6144]{1,2,0:T(8,128)} fusion(f32[]{:T(128)S(6)} %div.13, s32[768]{0:T(1024)S(1)} %iota_add_fusion.1, f32[768,6144]{0,1:T(8,128)} %get-tuple-element.108, f32[]{:T(128)S(6)} %div.12), kind=kLoop, calls=%fused_computation.255 | loop fusion | flops 18874368 | bytes 37751816 | tf_op jit(solution)/shard_map/broadcast_in_dim | solution.py:104
  587.1 18.7 %copy.44 = f32[1,768,6144]{2,1,0:T(8,128)} copy(f32[1,768,6144]{1,2,0:T(8,128)} %fusion.138) | data formatting | bytes 37748736
  605.8 71.4 %all-reduce.8.cloned.1.call-done = (f32[768,768]{0,1:T(8,128)}, f32[768,768]{0,1:T(8,128)}) async-done(((f32[768,768]{0,1:T(8,128)}, f32[768,768]{0,1:T(8,128)}), (f32[768,768]{0,1:T(8,128)}, f32[768,768]{0,1:T(8,128)})) %all-reduce.8.cloned.1.call-update) | async-done | bytes 4718608 | tf_op jit(solution)/shard_map/psum | solution.py:14
  677.2 8.7 convolution_subtract_fusion
  685.9 2.3 copy.42
  688.3 2.0 fusion
  691.6 11.7 %cholesky.563 = f32[128,128]{1,0:T(8,128)S(1)} custom-call(f32[128,128]{1,0:T(8,128)S(1)} %cholesky.692), custom_call_target="Cholesky" | custom-call | tf_op jit(solution)/shard_map/jit(cholesky)/cholesky | solution.py:97
  703.5 9.8 %custom-call.47 = f32[1,128,128]{1,2,0:T(8,128)S(1)} custom-call(f32[1,128,128]{2,1,0:T(8,128)S(1)} %get-tuple-element.90), custom_call_target="InvertDiagBlocksLowerTriangular" | custom-call | tf_op jit(solution)/shard_map/jit(cholesky)/cholesky | solution.py:97
  716.2 11.7 %cholesky.582 = f32[128,128]{1,0:T(8,128)S(1)} custom-call(f32[128,128]{1,0:T(8,128)S(1)} %cholesky.696), custom_call_target="Cholesky" | custom-call | tf_op jit(solution)/shard_map/jit(cholesky)/cholesky | solution.py:97
  729.3 9.9 %custom-call.48 = f32[1,128,128]{1,2,0:T(8,128)S(1)} custom-call(f32[1,128,128]{2,1,0:T(8,128)S(1)} %get-tuple-element.87), custom_call_target="InvertDiagBlocksLowerTriangular" | custom-call | tf_op jit(solution)/shard_map/jit(cholesky)/cholesky | solution.py:97
  741.2 11.7 %cholesky.603 = f32[128,128]{1,0:T(8,128)S(1)} custom-call(f32[128,128]{1,0:T(8,128)S(1)} %cholesky.701), custom_call_target="Cholesky" | custom-call | tf_op jit(solution)/shard_map/jit(cholesky)/cholesky | solution.py:97
  753.6 9.8 %custom-call.49 = f32[1,128,128]{1,2,0:T(8,128)S(1)} custom-call(f32[1,128,128]{2,1,0:T(8,128)S(1)} %get-tuple-element.84), custom_call_target="InvertDiagBlocksLowerTriangular" | custom-call | tf_op jit(solution)/shard_map/jit(cholesky)/cholesky | solution.py:97
  765.3 11.9 %cholesky.622 = f32[128,128]{1,0:T(8,128)S(1)} custom-call(f32[128,128]{1,0:T(8,128)S(1)} %cholesky.706), custom_call_target="Cholesky" | custom-call | tf_op jit(solution)/shard_map/jit(cholesky)/cholesky | solution.py:97
  777.8 9.8 %custom-call.50 = f32[1,128,128]{1,2,0:T(8,128)S(1)} custom-call(f32[1,128,128]{2,1,0:T(8,128)S(1)} %get-tuple-element.81), custom_call_target="InvertDiagBlocksLowerTriangular" | custom-call | tf_op jit(solution)/shard_map/jit(cholesky)/cholesky | solution.py:97
  789.4 11.7 %cholesky.641 = f32[128,128]{1,0:T(8,128)S(1)} custom-call(f32[128,128]{1,0:T(8,128)S(1)} %cholesky.711), custom_call_target="Cholesky" | custom-call | tf_op jit(solution)/shard_map/jit(cholesky)/cholesky | solution.py:97
  801.8 9.8 %custom-call.51 = f32[1,128,128]{1,2,0:T(8,128)S(1)} custom-call(f32[1,128,128]{2,1,0:T(8,128)S(1)} %get-tuple-element.78), custom_call_target="InvertDiagBlocksLowerTriangular" | custom-call | tf_op jit(solution)/shard_map/jit(cholesky)/cholesky | solution.py:97
  813.2 12.1 %cholesky.658 = f32[128,128]{1,0:T(8,128)S(1)} custom-call(f32[128,128]{1,0:T(8,128)S(1)} %convolution_subtract_fusion.17), custom_call_target="Cholesky" | custom-call | tf_op jit(solution)/shard_map/jit(cholesky)/cholesky | solution.py:97
  831.4 17.8 %while.5 = (s32[]{:T(128)}, f32[768,768]{1,0:T(8,128)}, s32[6,2]{0,1:T(2,128)S(1)}, f32[6,128,128]{2,1,0:T(8,128)S(1)}, s32[]{:T(128)}) while((s32[]{:T(128)}, f32[768,768]{1,0:T(8,128)}, s32[6,2]{0,1:T(2,128)S(1)}, f32[6,128,128]{2,1,0:T(8,128)S(1)}, s32[]{:T(128)}) %tuple.102), condition=%wide.while_cond.clone, body=%wide.while_body.clone.sunk | while | flops 2 | bytes 131181 | solution.py:98
  832.1 2.3 bitcast_dynamic-update-slice_fusion.5
  835.0 2.3 bitcast_dynamic-update-slice_fusion.5
  838.0 2.3 bitcast_dynamic-update-slice_fusion.5
  841.0 2.3 bitcast_dynamic-update-slice_fusion.5
  844.0 2.3 bitcast_dynamic-update-slice_fusion.5
  847.0 2.2 bitcast_dynamic-update-slice_fusion.5
  849.2 59.0 %custom-call.52 = f32[6,128,128]{1,2,0:T(8,128)S(1)} custom-call(f32[6,128,128]{2,1,0:T(8,128)S(1)} %get-tuple-element.19), custom_call_target="InvertDiagBlocksLowerTriangular" | custom-call | tf_op jit(solution)/shard_map/jit(_solve_triangular)/triangular_solve | solution.py:98
  908.2 9.0 subtract_bitcast_fusion
  924.0 2.0 fusion.20
  926.5 2.3 convolution_subtract_fusion.1
  931.0 2.4 maximum_bitcast_fusion
  933.4 6.1 copy.45
  (145 shorter events, 66.3 us)
Async XLA Ops:
  7.2 1.1 copy-start
  7.2 203.5 %all-gather.2.cloned.1.call-start = ((), (), s32[]{:S(2)}) async-start(), calls=%async_computation.2 | async-start | bytes 21233664 | tf_op jit(solution)/shard_map/all_gather | solution.py:48
  42.3 4.1 copy-start.8
  43.0 7.8 all-to-all-start.1
  46.2 286.2 %all-reduce.6.cloned.1.call-start = ((), (), s32[]{:S(2)}) async-start(), calls=%async_computation.3 | async-start | bytes 4718592 | tf_op jit(solution)/shard_map/psum | solution.py:14
  257.6 6.5 copy-start.2
  267.5 409.7 %all-reduce.8.cloned.1.call-start = ((), (), s32[]{:S(2)}) async-start(), calls=%async_computation.4 | async-start | bytes 9437184 | tf_op jit(solution)/shard_map/psum | solution.py:14
  332.4 3.7 copy-start.4
  338.1 1.5 copy-start.7
  496.2 62.5 %copy-start.5 = (f32[768,768]{1,0:T(8,128)S(1)}, f32[768,768]{1,0:T(8,128)}, u32[]{:S(2)}) copy-start(f32[768,768]{1,0:T(8,128)} %get-tuple-element.53) | copy-start | bytes 7077892
  690.2 1.4 copy-start.6
  929.3 1.7 copy-start.3
  933.4 6.1 copy-start.1
Sparse Core Ops, SparseCore 0:
  42.4 168.2 all-gather.1
  267.6 64.7 all-reduce.5
  571.2 105.9 all-reduce.7
where the time goes:
time: 955 us; the launch traced here: 946 us
  other arithmetic  407 us (43%)
  waiting for transfers between devices  283 us (30%)
  matrix products  86.9 us (9%)
  local copies, waits for them, and re-layouts  78.9 us (8%)
  blocking collectives  62.3 us (7%)
  between operations  24.1 us (3%)
    another operation x45, other arithmetic, local(): diagonal_factor = jnp.linalg.cholesky(diagonal_block)  248 us
    all_gather x1, waiting for transfers between devices, local(): lax.all_gather(received_rows.reshape(group_count * capacity, feature_widt...  144 us
    psum x2, waiting for transfers between devices, from_root(): return lax.psum(kept, axis)  136 us
    another operation x5, other arithmetic, local(): jax.scipy.linalg.solve_triangular(diagonal_factor, panel_block.T, lower=T...  121 us
    unnamed x23, local copies, waits for them, and re-layouts  36.4 us
    another operation x39, local copies, waits for them, and re-layouts, local(): jax.scipy.linalg.solve_triangular(diagonal_factor, panel_block.T, lower=T...  35.2 us
    all_to_all x1, blocking collectives, local(): lax.all_to_all(send_rows, 'expert', split_axis=0, concat_axis=0, tiled=True)  33.3 us
    another operation x22, matrix products, local(): jax.scipy.linalg.solve_triangular(diagonal_factor, panel_block.T, lower=T...  25.2 us
  transfers between devices with their start and end apart: 4, of which 4 were waited for; matrix products, arithmetic and copies ran while one was open for 4% of the time, Pallas kernels for 0%

commit v1 on v0

v1 whole, which is shorter than its diff:
```python
import jax
import jax.numpy as jnp
from jax import lax
from jax.experimental import pallas as pl
from jax.experimental.pallas import tpu as pltpu
from jax.sharding import PartitionSpec as P

PANEL = 768
PANELS = 2
BLOCK = 128
EXTRA = 128

damp_fraction = 0.01
HIGHEST = lax.Precision.HIGHEST


def contract_rows(a, b):
    return lax.dot_general(
        a, b, (((0,), (0,)), ((), ())), precision=HIGHEST, preferred_element_type=jnp.float32
    )


def block_inverse(block):
    steps = BLOCK // 8
    sublane = lax.broadcasted_iota(jnp.int32, (8, BLOCK), 0)
    lane = lax.broadcasted_iota(jnp.int32, (8, BLOCK), 1)
    left = [block[8 * t : 8 * t + 8] for t in range(steps)]
    right = [jnp.where(lane == sublane + 8 * t, 1.0, 0.0).astype(jnp.float32) for t in range(steps)]
    for s in range(steps):
        rows_a, rows_i = left[s], right[s]
        columns = [
            jnp.broadcast_to(rows_a[:, 8 * s + m : 8 * s + m + 1], (8, BLOCK)) for m in range(8)
        ]
        for k in range(8):
            inv = lax.rsqrt(jnp.broadcast_to(columns[k][k : k + 1], (8, BLOCK)))
            scaled = columns[k] * inv
            below = jnp.where(sublane > k, scaled, 0.0)
            for m in range(k + 1, 8):
                columns[m] = columns[m] - below * jnp.broadcast_to(scaled[m : m + 1], (8, BLOCK))
            row_a = jnp.broadcast_to(rows_a[k : k + 1], (8, BLOCK)) * inv
            row_i = jnp.broadcast_to(rows_i[k : k + 1], (8, BLOCK)) * inv
            rows_a = jnp.where(sublane == k, row_a, rows_a - below * row_a)
            rows_i = jnp.where(sublane == k, row_i, rows_i - below * row_i)
        left[s], right[s] = rows_a, rows_i
        if s < steps - 1:
            update = contract_rows(rows_a, jnp.concatenate([rows_a, rows_i], axis=1))
            for t in range(s + 1, steps):
                left[t] = left[t] - update[8 * t : 8 * t + 8, :BLOCK]
                right[t] = right[t] - update[8 * t : 8 * t + 8, BLOCK:]
    return jnp.concatenate(right, axis=0)


def inverse_kernel(a_ref, out_ref, w_ref):
    n = w_ref.shape[0]
    blocks = n // BLOCK
    width = n + BLOCK
    pltpu.sync_copy(a_ref, w_ref.at[:, pl.ds(0, n)])
    row = lax.broadcasted_iota(jnp.int32, (BLOCK, n), 0)
    column = lax.broadcasted_iota(jnp.int32, (BLOCK, n), 1)

    @pl.loop(0, blocks)
    def _(b):
        start = pl.multiple_of(b * BLOCK, BLOCK)
        w_ref[pl.ds(start, BLOCK), pl.ds(n, n)] = jnp.where(
            row + start == column, 1.0, 0.0
        ).astype(jnp.float32)

    @pl.loop(0, blocks)
    def _(b):
        start = pl.multiple_of(b * BLOCK, BLOCK)
        rows = pl.ds(start, BLOCK)
        inverse = block_inverse(w_ref[rows, rows])
        w_ref[rows, pl.ds(start, width)] = jnp.dot(
            inverse,
            w_ref[rows, pl.ds(start, width)],
            precision=HIGHEST,
            preferred_element_type=jnp.float32,
        )

        @pl.loop(b + 1, blocks)
        def _(i):
            below = pl.ds(pl.multiple_of(i * BLOCK, BLOCK), BLOCK)
            w_ref[below, pl.ds(start, width)] = w_ref[below, pl.ds(start, width)] - contract_rows(
                w_ref[rows, below], w_ref[rows, pl.ds(start, width)]
            )

    pltpu.sync_copy(w_ref.at[:, pl.ds(n, n)], out_ref)


def cholesky_inverse(matrix):
    n = matrix.shape[0]
    return pl.pallas_call(
        inverse_kernel,
        out_shape=jax.ShapeDtypeStruct((n, n), jnp.float32),
        in_specs=[pl.BlockSpec(memory_space=pl.ANY)],
        out_specs=pl.BlockSpec(memory_space=pl.ANY),
        scratch_shapes=[pltpu.VMEM((n, 2 * n), jnp.float32)],
        compiler_params=pltpu.CompilerParams(vmem_limit_bytes=48 * 1024 * 1024),
        cost_estimate=pl.CostEstimate(
            flops=24 * n * n * n, bytes_accessed=8 * n * n, transcendentals=0
        ),
        name="cholesky_inverse",
    )(matrix)


def local(activations, expert_ids):
    tile_count = lax.axis_size("tile")
    tokens, feature_width = activations.shape
    rows_device = feature_width // tile_count
    tile_index = lax.axis_index("tile")
    expert = lax.axis_index("expert")
    width = PANELS * PANEL
    axes = ("expert", "tile")

    features = activations.astype(jnp.float32)
    norm = jnp.sum(features * features, axis=1, keepdims=True)
    high = lax.reduce_precision(norm, 8, 7)
    middle = lax.reduce_precision(norm - high, 8, 7)
    low = norm - high - middle
    side = jnp.concatenate([expert_ids.astype(jnp.float32), high, middle, low], axis=1)
    side = jnp.pad(side, ((0, 0), (0, EXTRA - side.shape[1]))).astype(jnp.bfloat16)
    first = lax.all_gather(
        jnp.concatenate([activations[:, :width], side], axis=1), axes, axis=0, tiled=True
    )
    rest_own, first = lax.optimization_barrier((activations[:, width:], first))
    rest = lax.all_gather(rest_own, axes, axis=0, tiled=True)

    top = expert_ids.shape[1]
    sides = first[:, width:].astype(jnp.float32)
    panel_features = first[:, :width]
    mask = jnp.any(sides[:, :top] == expert.astype(jnp.float32), axis=1)
    count = jnp.sum(mask.astype(jnp.float32))
    scale = 2.0 / count
    norms = jnp.sum(sides[:, top : top + 3], axis=1)
    trace = jnp.sum(jnp.where(mask, norms, 0.0)) * scale
    damping = damp_fraction * trace / feature_width

    def masked(part):
        return jnp.where(mask[:, None], part, jnp.bfloat16(0))

    def gram(a, b):
        return jnp.einsum("tr,tc->rc", a, b, preferred_element_type=jnp.float32)

    leading = gram(masked(panel_features), panel_features) * scale
    position = jnp.arange(width, dtype=jnp.int32)
    leading = leading + jnp.where(position[:, None] == position[None, :], damping, 0.0)
    inverse = cholesky_inverse(leading)

    start = tile_index * rows_device
    in_first = start < width
    own = jnp.where(
        in_first,
        lax.dynamic_slice_in_dim(panel_features, jnp.where(in_first, start, 0), rows_device, 1),
        lax.dynamic_slice_in_dim(rest, jnp.where(in_first, 0, start - width), rows_device, 1),
    )
    own = masked(own)
    hessian = jnp.concatenate([gram(own, panel_features), gram(own, rest)], axis=1) * scale
    global_rows = start + jnp.arange(rows_device, dtype=jnp.int32)
    columns = jnp.arange(feature_width, dtype=jnp.int32)
    hessian = hessian + jnp.where(global_rows[:, None] == columns[None, :], damping, 0.0)
    panels = lax.dot_general(
        hessian[:, :width], inverse, (((1,), (1,)), ((), ())), precision=HIGHEST
    )
    panels = jnp.where(global_rows[:, None] >= position[None, :], panels, 0.0)
    return (hessian[None], panels[None])


def solution(mesh):
    placed = (P(("expert", "tile"), None), P(("expert", "tile"), None))
    return jax.shard_map(
        local,
        mesh=mesh,
        in_specs=placed,
        out_specs=(P("expert", "tile", None), P("expert", "tile", None)),
        check_vma=False,
    )
```

time: 955 us -> 347 us (0.36)
  other arithmetic: 407 us -> 12.6 us
  waiting for transfers between devices: 283 us -> 66.4 us
  Pallas kernels: 0 us -> 180 us
  local copies, waits for them, and re-layouts: 78.9 us -> 7.68 us
  blocking collectives: 62.3 us -> 0 us
  matrix products: 86.9 us -> 64.7 us
    another operation x51 -> x2, other arithmetic: 369 us -> 0.69 us  [the longest x45 248 us: local(): diagonal_factor = jnp.linalg.cholesky(diagonal_block)]
    pallas_call x0 -> x1, Pallas kernels: none -> 180 us  [cholesky_inverse(): pl.pallas_call(inverse_kernel, out_shape=jax.ShapeDtypeStruct((n, n), jnp...]
    psum x2 -> x0, waiting for transfers between devices: 136 us -> none  [from_root(): return lax.psum(kept, axis)]
    all_gather x1 -> x2, waiting for transfers between devices: 144 us -> 66.4 us  [the longest x1 66.4 us: local(): lax.all_gather(jnp.concatenate([activations[:, :width], side], axis=1), a...]
    another operation x42 -> x0, matrix products: 44.8 us -> none  [the longest x22 25.2 us: local(): jax.scipy.linalg.solve_triangular(diagonal_factor, panel_block.T, lower=T...]
    unnamed x23 -> x3, local copies, waits for them, and re-layouts: 36.4 us -> 0.11 us
    another operation x51 -> x0, local copies, waits for them, and re-layouts: 35.6 us -> none  [the longest x39 35.2 us: local(): jax.scipy.linalg.solve_triangular(diagonal_factor, panel_block.T, lower=T...]
    all_to_all x1 -> x0, blocking collectives: 33.3 us -> none  [local(): lax.all_to_all(send_rows, 'expert', split_axis=0, concat_axis=0, tiled=True)]
  transfers between devices with their start and end apart: 4 -> 2, of which waited for: 4 -> 1; matrix products, arithmetic and copies ran while one was open for 4% -> 7% of each run, Pallas kernels for 0% -> 52%
where the time goes in v1:
time: 347 us
  Pallas kernels  180 us (52%)
  waiting for transfers between devices  66.4 us (19%)
  matrix products  64.7 us (19%)
  between operations  15.5 us (4%)
  other arithmetic  12.6 us (4%)
  local copies, waits for them, and re-layouts  7.68 us (2%)
    pallas_call x1, Pallas kernels, cholesky_inverse(): pl.pallas_call(inverse_kernel, out_shape=jax.ShapeDtypeStruct((n, n), jnp...  180 us
    all_gather x1, waiting for transfers between devices, local(): lax.all_gather(jnp.concatenate([activations[:, :width], side], axis=1), a...  66.4 us
    dot_general x3, matrix products, gram(): return jnp.einsum('tr,tc->rc', a, b, preferred_element_type=jnp.float32)  36.9 us
    dot_general x1, matrix products, local(): lax.dot_general(hessian[:, :width], inverse, (((1,), (1,)), ((), ())), pr...  27.8 us
    add x1, other arithmetic, local(): hessian + jnp.where(global_rows[:, None] == columns[None, :], damping, 0.0)  7.42 us
  transfers between devices with their start and end apart: 2, of which 1 were waited for; matrix products, arithmetic and copies ran while one was open for 7% of the time, Pallas kernels for 52%

profile of v1, /device:TPU:0, one launch (start us, length us, event | category | flops | bytes accessed | tf_op | source)
XLA Modules:
  0.0 346.7 jit_solution(3854457996851536768)
XLA Ops:
  7.2 0.0 all-gather.3.cloned.1.call-start
  7.2 1.3 multiply_reduce_fusion
  8.5 0.9 slice.22
  9.4 0.7 convert_convert_fusion
  10.1 0.1 copy.5
  10.2 0.7 fusion.19
  10.9 0.0 all-gather.3.cloned.1.call-update
  11.0 0.0 all-gather.5.cloned.1.call-start
  11.0 1.8 slice.21
  12.8 66.4 %all-gather.3.cloned.1.call-done = bf16[1536,1664]{1,0:T(8,128)(2,1)} async-done(((bf16[48,1664]{1,0:T(8,128)(2,1)}), bf16[1536,1664]{1,0:T(8,128)(2,1)}) %all-gather.3.cloned.1.call-update) | async-done | bytes 5111824 | tf_op jit(solution)/shard_map/all_gather | solution.py:122
  79.2 0.0 all-gather.5.cloned.1.call-update
  79.2 4.8 %slice.25 = bf16[1536,1536]{1,0:T(8,128)(2,1)} slice(bf16[1536,1664]{1,0:T(8,128)(2,1)} %all-gather.3.cloned.1.call-done), slice={[0:1536], [0:1536]} | slice | bytes 9437184 | tf_op jit(solution)/shard_map/slice | solution.py:130
  84.1 1.0 slice_convert_fusion
  85.1 0.5 slice_reduce_fusion
  85.6 0.3 fusion.17
  85.9 0.7 convert_reduce_fusion
  88.0 14.6 %select_add_fusion.a_ref = f32[1536,1536]{1,0:T(8,128)} fusion(f32[]{:T(128)S(6)} %div.7, f32[]{:T(128)S(6)} %div.6, pred[1536]{0:T(1024)(128)(4,1)S(1)} %fusion.17, bf16[1536,1664]{1,0:T(8,128)(2,1)} %all-gather.3.cloned.1.call-done), kind=kOutput, calls=%fused_computation.4 | convolution fusion | flops 7259553792 | bytes 18875912 | tf_op jit(solution)/shard_map/tr,tc->rc/dot_general | solution.py:142
  102.6 179.8 %cholesky_inverse.1 = f32[1536,1536]{1,0:T(8,128)} custom-call(f32[1536,1536]{1,0:T(8,128)} %select_add_fusion.a_ref), custom_call_target="tpu_custom_call" | custom-call | flops 86973087744 | bytes 18874368 | tf_op jit(solution)/shard_map/cholesky_inverse/pallas_call | solution.py:92
  282.3 0.0 all-gather.5.cloned.1.call-done
  282.3 0.0 copy-start
  282.3 16.4 %fusion.25 = f32[768,4608]{1,0:T(8,128)S(1)} fusion(bf16[1536,4608]{1,0:T(8,128)(2,1)} %all-gather.5.cloned.1.call-done, s32[]{:T(128)S(6)} %select_n.59, bf16[1536,1536]{1,0:T(8,128)(2,1)} %slice.25, s32[]{:T(128)S(6)} %select_n.57, pred[1536]{0:T(1024)(128)(4,1)S(1)} %fusion.17, pred[]{:T(512)S(6)} %lt.9), kind=kOutput, calls=%fused_computation.46 | convolution fusion | flops 10873995264 | bytes 33031688 | tf_op jit(solution)/shard_map/tr,tc->rc/dot_general | solution.py:142
  298.8 0.0 copy-done
  298.8 5.9 %fusion.26 = f32[768,1536]{1,0:T(8,128)S(1)} fusion(bf16[1536,1536]{1,0:T(8,128)(2,1)S(1)} %copy-done, bf16[1536,4608]{1,0:T(8,128)(2,1)} %all-gather.5.cloned.1.call-done, s32[]{:T(128)S(6)} %select_n.59, s32[]{:T(128)S(6)} %select_n.57, pred[1536]{0:T(1024)(128)(4,1)S(1)} %fusion.17, pred[]{:T(512)S(6)} %lt.9), kind=kOutput, calls=%fused_computation.47 | convolution fusion | flops 3626237952 | bytes 14157833 | tf_op jit(solution)/shard_map/tr,tc->rc/dot_general | solution.py:142
  304.7 27.8 %select_bitcast_fusion = f32[1,768,1536]{2,1,0:T(8,128)} fusion(f32[1536,1536]{1,0:T(8,128)} %cholesky_inverse.1, f32[768,4608]{1,0:T(8,128)S(1)} %fusion.25, f32[768,1536]{1,0:T(8,128)S(1)} %fusion.26, f32[]{:T(128)S(6)} %div.7, f32[]{:T(128)S(6)} %div.6, s32[768]{0:T(1024)S(1)} %iota_add_fusion), kind=kOutput, calls=%fused_computation.13 | convolution fusion | flops 21752709120 | bytes 33033224 | tf_op jit(solution)/shard_map/dot_general | solution.py:161
  332.5 7.4 %fusion = f32[1,768,6144]{2,1,0:T(8,128)} fusion(f32[1,768,4608]{2,1,0:T(8,128)S(1)} %bitcast.14, f32[1,768,1536]{2,1,0:T(8,128)S(1)} %bitcast.15, f32[]{:T(128)S(6)} %div.7, s32[768]{0:T(1024)S(1)} %iota_add_fusion, f32[]{:T(128)S(6)} %div.6), kind=kLoop, calls=%fused_computation.1 | loop fusion | flops 23592960 | bytes 37751816 | tf_op jit(solution)/shard_map/add | solution.py:160
  (3 shorter events, 0.0 us)
Async XLA Ops:
  7.2 72.0 %all-gather.3.cloned.1.call-start = ((), (), s32[]{:S(2)}) async-start(), calls=%async_computation | async-start | bytes 5271552 | tf_op jit(solution)/shard_map/all_gather | solution.py:122
  11.0 271.4 %all-gather.5.cloned.1.call-start = ((), (), s32[]{:S(2)}) async-start(), calls=%async_computation.1 | async-start | bytes 14598144 | tf_op jit(solution)/shard_map/all_gather | solution.py:126
  282.3 16.4 %copy-start = (bf16[1536,1536]{1,0:T(8,128)(2,1)S(1)}, bf16[1536,1536]{1,0:T(8,128)(2,1)}, u32[]{:S(2)}) copy-start(bf16[1536,1536]{1,0:T(8,128)(2,1)} %slice.25) | copy-start | bytes 14155780
Sparse Core Ops, SparseCore 0:
  11.6 67.5 all-gather.2
  82.2 102.6 all-gather.4

commit v2 on v1

--- a/solution.py
+++ b/solution.py
@@ -26,31 +26,63 @@
     lane = lax.broadcasted_iota(jnp.int32, (8, BLOCK), 1)
     left = [block[8 * t : 8 * t + 8] for t in range(steps)]
     right = [jnp.where(lane == sublane + 8 * t, 1.0, 0.0).astype(jnp.float32) for t in range(steps)]
+
+    def spread(tile, s):
+        return [jnp.broadcast_to(tile[:, 8 * s + m : 8 * s + m + 1], (8, BLOCK)) for m in range(8)]
+
+    def row_of(tile, k):
+        return jnp.broadcast_to(tile[k : k + 1], (8, BLOCK))
+
     for s in range(steps):
         rows_a, rows_i = left[s], right[s]
-        columns = [
-            jnp.broadcast_to(rows_a[:, 8 * s + m : 8 * s + m + 1], (8, BLOCK)) for m in range(8)
-        ]
+        columns = spread(rows_a, s)
+        ahead = s + 1 < steps
+        if ahead:
+            next_a, next_i = left[s + 1], right[s + 1]
+            next_columns = spread(next_a, s)
         for k in range(8):
-            inv = lax.rsqrt(jnp.broadcast_to(columns[k][k : k + 1], (8, BLOCK)))
-            scaled = columns[k] * inv
-            below = jnp.where(sublane > k, scaled, 0.0)
+            inv = lax.rsqrt(row_of(columns[k], k))
+            square = inv * inv
+            entries = [row_of(columns[k], m) if m > k else None for m in range(8)]
+            below = jnp.where(sublane > k, columns[k], 0.0)
             for m in range(k + 1, 8):
-                columns[m] = columns[m] - below * jnp.broadcast_to(scaled[m : m + 1], (8, BLOCK))
-            row_a = jnp.broadcast_to(rows_a[k : k + 1], (8, BLOCK)) * inv
-            row_i = jnp.broadcast_to(rows_i[k : k + 1], (8, BLOCK)) * inv
-            rows_a = jnp.where(sublane == k, row_a, rows_a - below * row_a)
-            rows_i = jnp.where(sublane == k, row_i, rows_i - below * row_i)
+                columns[m] = columns[m] - (below * entries[m]) * square
+            row_a = row_of(rows_a, k) * inv
+            row_i = row_of(rows_i, k) * inv
+            factor = below * inv
+            rows_a = jnp.where(sublane == k, row_a, rows_a - factor * row_a)
+            rows_i = jnp.where(sublane == k, row_i, rows_i - factor * row_i)
+            if ahead:
+                factor = next_columns[k] * inv
+                for m in range(k + 1, 8):
+                    next_columns[m] = next_columns[m] - factor * (entries[m] * inv)
+                next_a = next_a - factor * row_a
+                next_i = next_i - factor * row_i
         left[s], right[s] = rows_a, rows_i
-        if s < steps - 1:
+        if ahead:
+            left[s + 1], right[s + 1] = next_a, next_i
+        if s + 2 < steps:
             update = contract_rows(rows_a, jnp.concatenate([rows_a, rows_i], axis=1))
-            for t in range(s + 1, steps):
+            for t in range(s + 2, steps):
                 left[t] = left[t] - update[8 * t : 8 * t + 8, :BLOCK]
                 right[t] = right[t] - update[8 * t : 8 * t + 8, BLOCK:]
     return jnp.concatenate(right, axis=0)
 
 
-def inverse_kernel(a_ref, out_ref, w_ref):
+def three_terms(value):
+    high = value.astype(jnp.bfloat16)
+    rest = value - high.astype(jnp.float32)
+    middle = rest.astype(jnp.bfloat16)
+    low = (rest - middle.astype(jnp.float32)).astype(jnp.bfloat16)
+    return high, middle, low
+
+
+def stacked_left(value):
+    h, m, l = three_terms(value)
+    return jnp.concatenate([h, h, m, m, h, l], axis=1)
+
+
+def inverse_kernel(a_ref, out_ref, w_ref, terms_ref):
     n = w_ref.shape[0]
     blocks = n // BLOCK
     width = n + BLOCK
@@ -65,23 +97,31 @@
             row + start == column, 1.0, 0.0
         ).astype(jnp.float32)
 
+    def store_terms(value):
+        h, m, l = three_terms(value)
+        for place, term in enumerate((h, m, h, m, l, h)):
+            terms_ref[pl.ds(place * BLOCK, BLOCK), :] = term
+
     @pl.loop(0, blocks)
     def _(b):
         start = pl.multiple_of(b * BLOCK, BLOCK)
         rows = pl.ds(start, BLOCK)
+        window = pl.ds(start, width)
         inverse = block_inverse(w_ref[rows, rows])
-        w_ref[rows, pl.ds(start, width)] = jnp.dot(
-            inverse,
-            w_ref[rows, pl.ds(start, width)],
-            precision=HIGHEST,
-            preferred_element_type=jnp.float32,
+        store_terms(w_ref[rows, window])
+        scaled = jnp.dot(
+            stacked_left(inverse), terms_ref[...], preferred_element_type=jnp.float32
         )
+        w_ref[rows, window] = scaled
+        store_terms(scaled)
 
         @pl.loop(b + 1, blocks)
         def _(i):
             below = pl.ds(pl.multiple_of(i * BLOCK, BLOCK), BLOCK)
-            w_ref[below, pl.ds(start, width)] = w_ref[below, pl.ds(start, width)] - contract_rows(
-                w_ref[rows, below], w_ref[rows, pl.ds(start, width)]
+            w_ref[below, window] = w_ref[below, window] - jnp.dot(
+                stacked_left(w_ref[rows, below].T),
+                terms_ref[...],
+                preferred_element_type=jnp.float32,
             )
 
     pltpu.sync_copy(w_ref.at[:, pl.ds(n, n)], out_ref)
@@ -94,13 +134,62 @@
         out_shape=jax.ShapeDtypeStruct((n, n), jnp.float32),
         in_specs=[pl.BlockSpec(memory_space=pl.ANY)],
         out_specs=pl.BlockSpec(memory_space=pl.ANY),
-        scratch_shapes=[pltpu.VMEM((n, 2 * n), jnp.float32)],
+        scratch_shapes=[
+            pltpu.VMEM((n, 2 * n), jnp.float32),
+            pltpu.VMEM((6 * BLOCK, n + BLOCK), jnp.bfloat16),
+        ],
         compiler_params=pltpu.CompilerParams(vmem_limit_bytes=48 * 1024 * 1024),
         cost_estimate=pl.CostEstimate(
             flops=24 * n * n * n, bytes_accessed=8 * n * n, transcendentals=0
         ),
         name="cholesky_inverse",
     )(matrix)
+
+
+def hessian_kernel(lead, numbers_ref, own_ref, first_ref, rest_ref, out_ref):
+    step = pl.program_id(0)
+    rows, columns = out_ref.shape
+    scale, damping, start = numbers_ref[0], numbers_ref[1], numbers_ref[2]
+    row = lax.broadcasted_iota(jnp.int32, (rows, columns), 0) + start.astype(jnp.int32)
+    column = lax.broadcasted_iota(jnp.int32, (rows, columns), 1) + step * columns
+
+    def finish(part_ref):
+        total = jnp.dot(own_ref[...], part_ref[...], preferred_element_type=jnp.float32)
+        out_ref[...] = total * scale + jnp.where(row == column, damping, 0.0)
+
+    @pl.when(step < lead)
+    def _():
+        finish(first_ref)
+
+    @pl.when(step >= lead)
+    def _():
+        finish(rest_ref)
+
+
+def hessian_rows(numbers, own, first, rest, width):
+    rows, tokens = own.shape
+    block = 512
+    lead = width // block
+    steps = lead + rest.shape[1] // block
+    return pl.pallas_call(
+        lambda *refs: hessian_kernel(lead, *refs),
+        grid=(steps,),
+        out_shape=jax.ShapeDtypeStruct((rows, steps * block), jnp.float32),
+        in_specs=[
+            pl.BlockSpec(memory_space=pltpu.SMEM),
+            pl.BlockSpec((rows, tokens), lambda j: (0, 0)),
+            pl.BlockSpec((tokens, block), lambda j: (0, jnp.minimum(j, lead - 1))),
+            pl.BlockSpec((tokens, block), lambda j: (0, jnp.maximum(j - lead, 0))),
+        ],
+        out_specs=pl.BlockSpec((rows, block), lambda j: (0, j)),
+        compiler_params=pltpu.CompilerParams(vmem_limit_bytes=56 * 1024 * 1024),
+        cost_estimate=pl.CostEstimate(
+            flops=2 * rows * tokens * steps * block,
+            bytes_accessed=4 * rows * steps * block + 2 * tokens * steps * block,
+            transcendentals=0,
+        ),
+        name="hessian_rows",
+    )(numbers, own, first, rest)
 
 
 def local(activations, expert_ids):
@@ -119,9 +208,9 @@
     low = norm - high - middle
     side = jnp.concatenate([expert_ids.astype(jnp.float32), high, middle, low], axis=1)
     side = jnp.pad(side, ((0, 0), (0, EXTRA - side.shape[1]))).astype(jnp.bfloat16)
-    first = lax.all_gather(
-        jnp.concatenate([activations[:, :width], side], axis=1), axes, axis=0, tiled=True
-    )
+    first = jnp.concatenate([activations[:, :width], side], axis=1)
+    for axis in ("tile", "expert"):
+        first = lax.all_gather(first, axis, axis=0, tiled=True)
     rest_own, first = lax.optimization_barrier((activations[:, width:], first))
     rest = lax.all_gather(rest_own, axes, axis=0, tiled=True)
 
@@ -153,14 +242,23 @@
         lax.dynamic_slice_in_dim(panel_features, jnp.where(in_first, start, 0), rows_device, 1),
         lax.dynamic_slice_in_dim(rest, jnp.where(in_first, 0, start - width), rows_device, 1),
     )
-    own = masked(own)
-    hessian = jnp.concatenate([gram(own, panel_features), gram(own, rest)], axis=1) * scale
+    numbers = jnp.stack([scale, damping, start.astype(jnp.float32)])
+    hessian = hessian_rows(numbers, masked(own).T, first, rest, width)
     global_rows = start + jnp.arange(rows_device, dtype=jnp.int32)
-    columns = jnp.arange(feature_width, dtype=jnp.int32)
-    hessian = hessian + jnp.where(global_rows[:, None] == columns[None, :], damping, 0.0)
-    panels = lax.dot_general(
-        hessian[:, :width], inverse, (((1,), (1,)), ((), ())), precision=HIGHEST
-    )
+
+    pieces = []
+    for k in range(PANELS):
+        end = (k + 1) * PANEL
+        pieces.append(
+            lax.dot_general(
+                hessian[:, :end],
+                inverse[k * PANEL : end, :end],
+                (((1,), (1,)), ((), ())),
+                precision=lax.Precision.HIGH,
+                preferred_element_type=jnp.float32,
+            )
+        )
+    panels = jnp.concatenate(pieces, axis=1)
     panels = jnp.where(global_rows[:, None] >= position[None, :], panels, 0.0)
     return (hessian[None], panels[None])
 

time: 347 us -> 301 us (0.87)
  Pallas kernels: 180 us -> 143 us
  matrix products: 64.7 us -> 29 us
  waiting for transfers between devices: 66.4 us -> 85.9 us
  local copies, waits for them, and re-layouts: 7.68 us -> 16.1 us
    pallas_call x1, Pallas kernels: 180 us -> 119 us  [cholesky_inverse(): pl.pallas_call(inverse_kernel, out_shape=jax.ShapeDtypeStruct((n, n), jnp...]
    pallas_call x0 -> x1, Pallas kernels: none -> 24.2 us  [hessian_rows(): pl.pallas_call(lambda *refs: hessian_kernel(lead, *refs), grid=(steps,),...]
    dot_general x3 -> x1, matrix products: 36.9 us -> 14.5 us  [gram(): return jnp.einsum('tr,tc->rc', a, b, preferred_element_type=jnp.float32)]
    all_gather x1 -> x2, waiting for transfers between devices: 66.4 us -> 85.9 us  [local(): first = lax.all_gather(first, axis, axis=0, tiled=True)]
    dot_general x1 -> x2, matrix products: 27.8 us -> 14.4 us  [local(): lax.dot_general(hessian[:, :end], inverse[k * PANEL:end, :end], (((1,), (...]
    add x1 -> x0, other arithmetic: 7.42 us -> none  [local(): hessian + jnp.where(global_rows[:, None] == columns[None, :], damping, 0.0)]
    unnamed x3 -> x1, local copies, waits for them, and re-layouts: 0.11 us -> 6.04 us
  transfers between devices with their start and end apart: 2 -> 3, of which waited for: 1 -> 2; matrix products, arithmetic and copies ran while one was open for 7% -> 8% of each run, Pallas kernels for 52% -> 39%
where the time goes in v2:
time: 301 us; the launch traced here: 300 us
  Pallas kernels  143 us (48%)
  waiting for transfers between devices  85.9 us (29%)
  matrix products  29 us (10%)
  local copies, waits for them, and re-layouts  16.1 us (5%)
  between operations  15 us (5%)
  other arithmetic  11.3 us (4%)
    pallas_call x1, Pallas kernels, cholesky_inverse(): pl.pallas_call(inverse_kernel, out_shape=jax.ShapeDtypeStruct((n, n), jnp...  119 us
    all_gather x2, waiting for transfers between devices, local(): first = lax.all_gather(first, axis, axis=0, tiled=True)  85.9 us
    pallas_call x1, Pallas kernels, hessian_rows(): pl.pallas_call(lambda *refs: hessian_kernel(lead, *refs), grid=(steps,),...  24.2 us
    dot_general x1, matrix products, gram(): return jnp.einsum('tr,tc->rc', a, b, preferred_element_type=jnp.float32)  14.5 us
    dot_general x2, matrix products, local(): lax.dot_general(hessian[:, :end], inverse[k * PANEL:end, :end], (((1,), (...  14.4 us
    unnamed x1, local copies, waits for them, and re-layouts  6.04 us
  transfers between devices with their start and end apart: 3, of which 2 were waited for; matrix products, arithmetic and copies ran while one was open for 8% of the time, Pallas kernels for 39%

profile of v2, /device:TPU:0, one launch (start us, length us, event | category | flops | bytes accessed | tf_op | source)
XLA Modules:
  0.0 300.2 jit_solution(11797804758144947894)
XLA Ops:
  7.2 0.0 all-gather.4.cloned.1.call-start
  7.2 1.3 multiply_reduce_fusion
  8.5 0.9 slice.31
  9.4 0.7 convert_convert_fusion
  10.1 0.1 copy.9
  10.2 0.7 fusion.21
  10.9 0.0 all-gather.4.cloned.1.call-update
  11.0 0.0 all-gather.6.cloned.1.call-start
  11.0 26.0 %all-gather.4.cloned.1.call-done = bf16[384,1664]{1,0:T(8,128)(2,1)} async-done(((bf16[48,1664]{1,0:T(8,128)(2,1)}), bf16[384,1664]{1,0:T(8,128)(2,1)}) %all-gather.4.cloned.1.call-update) | async-done | bytes 1277968 | tf_op jit(solution)/shard_map/all_gather | solution.py:213
  37.0 0.0 all-gather.6.cloned.1.call-update
  37.0 0.0 all-gather.8.cloned.1.call-start
  37.1 1.8 slice.30
  38.9 59.9 %all-gather.6.cloned.1.call-done.refs_2_ = bf16[1536,1664]{1,0:T(8,128)(2,1)} async-done(((bf16[384,1664]{1,0:T(8,128)(2,1)}), bf16[1536,1664]{1,0:T(8,128)(2,1)}) %all-gather.6.cloned.1.call-update) | async-done | bytes 5111824 | tf_op jit(solution)/shard_map/all_gather | solution.py:213
  98.8 0.0 all-gather.8.cloned.1.call-update
  98.8 4.8 %slice.35 = bf16[1536,1536]{1,0:T(8,128)(2,1)} slice(bf16[1536,1664]{1,0:T(8,128)(2,1)} %all-gather.6.cloned.1.call-done.refs_2_), slice={[0:1536], [0:1536]} | slice | bytes 9437184 | tf_op jit(solution)/shard_map/slice | solution.py:219
  103.7 1.0 slice_convert_fusion
  104.7 0.5 slice_reduce_fusion
  105.2 0.3 fusion.19
  105.5 0.7 convert_reduce_fusion
  107.4 0.6 pad_maximum_fusion.1.refs_0_
  108.0 14.5 %select_add_fusion.a_ref = f32[1536,1536]{1,0:T(8,128)} fusion(f32[]{:T(128)} %div.7, f32[]{:T(128)} %div.6, pred[1536]{0:T(1024)(128)(4,1)S(1)} %fusion.19, bf16[1536,1664]{1,0:T(8,128)(2,1)} %all-gather.6.cloned.1.call-done.refs_2_), kind=kOutput, calls=%fused_computation.1 | convolution fusion | flops 7259553792 | bytes 18876928 | tf_op jit(solution)/shard_map/tr,tc->rc/dot_general | solution.py:231
  122.5 118.5 %cholesky_inverse.1 = f32[1536,1536]{1,0:T(8,128)} custom-call(f32[1536,1536]{1,0:T(8,128)} %select_add_fusion.a_ref), custom_call_target="tpu_custom_call" | custom-call | flops 86973087744 | bytes 18874368 | tf_op jit(solution)/shard_map/cholesky_inverse/pallas_call | solution.py:132
  241.0 0.0 all-gather.8.cloned.1.call-done.refs_3_
  241.0 2.9 select_bitcast_fusion
  244.0 2.4 copy.10.refs_1_
  246.4 24.2 %hessian_rows.1 = f32[768,6144]{1,0:T(8,128)} custom-call(f32[3]{0:T(128)} %pad_maximum_fusion.1.refs_0_, bf16[768,1536]{1,0:T(8,128)(2,1)} %copy.10.refs_1_, bf16[1536,1664]{1,0:T(8,128)(2,1)} %all-gather.6.cloned.1.call-done.refs_2_, bf16[1536,4608]{1,0:T(8,128)(2,1)} %all-gather.8.cloned.1.call-done.refs_3_), custom_call_target="tpu_custom_call" | custom-call | flops 14495514624 | bytes 37748736 | tf_op jit(solution)/shard_map/hessian_rows/pallas_call | solution.py:174
  270.6 5.4 %fusion.14 = f32[1,768,768]{1,2,0:T(8,128)S(1)} fusion(f32[1536,1536]{1,0:T(8,128)} %cholesky_inverse.1, f32[768,6144]{1,0:T(8,128)} %hessian_rows.1), kind=kOutput, calls=%fused_computation.16 | convolution fusion | flops 2717908992 | bytes 7077888 | tf_op jit(solution)/shard_map/dot_general | solution.py:253
  276.0 9.1 %fusion.9 = f32[1,768,768]{1,2,0:T(8,128)S(1)} fusion(f32[1536,1536]{1,0:T(8,128)} %cholesky_inverse.1, f32[768,6144]{1,0:T(8,128)} %hessian_rows.1), kind=kOutput, calls=%fused_computation.15 | convolution fusion | flops 5435817984 | bytes 11796480 | tf_op jit(solution)/shard_map/dot_general | solution.py:253
  285.0 2.6 maximum_select_fusion
  287.7 6.0 %copy.11 = f32[1,768,1536]{2,1,0:T(8,128)} copy(f32[1,768,1536]{1,2,0:T(8,128)} %maximum_select_fusion) | data formatting | bytes 9437184
  (3 shorter events, 0.0 us)
Async XLA Ops:
  7.2 29.9 %all-gather.4.cloned.1.call-start = ((), (), s32[]{:S(2)}) async-start(), calls=%async_computation | async-start | bytes 1437696 | tf_op jit(solution)/shard_map/all_gather | solution.py:213
  11.0 87.8 %all-gather.6.cloned.1.call-start = ((), (), s32[]{:S(2)}) async-start(), calls=%async_computation.1 | async-start | bytes 6389760 | tf_op jit(solution)/shard_map/all_gather | solution.py:213
  37.0 204.0 %all-gather.8.cloned.1.call-start = ((), (), s32[]{:S(2)}) async-start(), calls=%async_computation.2 | async-start | bytes 14598144 | tf_op jit(solution)/shard_map/all_gather | solution.py:215
Sparse Core Ops, SparseCore 0:
  11.1 25.9 all-gather.3
  38.9 59.8 all-gather.5
  101.8 103.3 all-gather.7
